TPU v7x, 32 devices: a whole 2x2x4 slice. The times are simulated.
32 devices in a mesh: cases: 2 (over y), gx: 4 (over z), gy: 2 (over x), af: 2 (over core).
Axes of the slice: x: 2, y: 2, z: 4, core: 2. Of those that a mesh axis runs over, the one named last changes fastest.
Arguments:
- state_zero: float32 [5, 4, 64, 256], P(None, 'af', ('cases', 'gx'), 'gy'), parts along dimension 2, may hold values from -4 to 17, as said below
- state_one: float32 [5, 4, 64, 256], P(None, 'af', ('cases', 'gx'), 'gy'), parts along dimension 2, may hold values from -4 to 17, as said below
- cotangent: float32 [5, 4, 64, 256], P(None, 'af', ('cases', 'gx'), 'gy'), parts along dimension 2, may hold values from -45 to 45
- weight_in: float32 [64, 5], replicated, may hold values from -2.5 to 2.5
- bias_in: float32 [64], replicated, may hold values from -3 to 3
- weight_out: float32 [5, 64], replicated, may hold values from -0.75 to 0.75
- bias_out: float32 [5], replicated, may hold values from -3 to 3
Outputs:
- grad_state: float32 [5, 4, 64, 256], P(None, 'af', ('cases', 'gx'), 'gy'), parts along dimension 2
- grad_weight_in: float32 [128, 5], P('cases'), parts along dimension 0
- grad_bias_in: float32 [128], P('cases'), parts along dimension 0
- grad_weight_out: float32 [10, 64], P('cases'), parts along dimension 0
- grad_bias_out: float32 [10], P('cases'), parts along dimension 0
There are 2 independent parts, one for each index of `cases`. A program takes and returns all parts, laid end to end along the dimension named above; an argument that names none is the same for every part. Nothing has to cross between parts.
Inputs may be any that keep to these rules, and one draw needn't show every extreme that they name: `state_zero`: field 0 (density) lies in 0.5 to 2, velocities (fields 1 to 3 over field 0) in -2 to 2 and pressure in 0.5 to 2 at every cell. `state_one`: field 0 (density) lies in 0.5 to 2, velocities (fields 1 to 3 over field 0) in -2 to 2 and pressure in 0.5 to 2 at every cell.
All inputs are finite; a program needn't handle non-finite values.
Results may differ from a plain program's by a relative error of at most 0.00016.
Values sent between devices are 32-bit elements; how exact they have to be, the bound alone decides.
A program may use at most 64 MiB of HBM per device.

v0:
```python
import jax
import jax.numpy as jnp
from jax import lax
from jax.sharding import PartitionSpec as P

GAMMA = 1.4
TIME_STEP = 0.1
VISCOSITY = 0.2
WENO_EPS = 1e-06


def padded_2(cells, sides, width):
    for axis, dim in sides:
        count = lax.axis_size(axis)
        head = lax.slice_in_dim(cells, 0, width, axis=dim)
        tail = lax.slice_in_dim(cells, cells.shape[dim] - width, cells.shape[dim], axis=dim)
        cells = jnp.concatenate(
            [
                lax.ppermute(tail, axis, [(i, (i + 1) % count) for i in range(count)]),
                cells,
                lax.ppermute(head, axis, [((i + 1) % count, i) for i in range(count)]),
            ],
            axis=dim,
        )
    return cells


def from_behind(array, axis, by):
    count = lax.axis_size(axis)
    return lax.ppermute(array, axis, [(i, (i + by) % count) for i in range(count)])


def pressure_of(fields):
    kinetic = (
        0.5 * (fields[1] * fields[1] + fields[2] * fields[2] + fields[3] * fields[3]) / fields[0]
    )
    return (GAMMA - 1.0) * (fields[4] - kinetic)


def max_speed(fields):
    density = fields[0]
    sound = jnp.sqrt(GAMMA * pressure_of(fields) / density)
    along = jnp.maximum(jnp.abs(fields[1] / density), jnp.abs(fields[2] / density))
    return jnp.max(along + sound)


def face_flux(fields, normal_index):
    pressure = pressure_of(fields)
    velocity = fields[normal_index + 1] / fields[0]
    parts = [
        fields[0] * velocity,
        fields[1] * velocity,
        fields[2] * velocity,
        fields[3] * velocity,
        (fields[4] + pressure) * velocity,
    ]
    parts[normal_index + 1] = parts[normal_index + 1] + pressure
    return jnp.stack(parts)


def weno_face(cell_a, cell_b, cell_c, cell_d, cell_e):
    smooth_a = (
        13.0 / 12.0 * (cell_a - 2.0 * cell_b + cell_c) ** 2
        + 0.25 * (cell_a - 4.0 * cell_b + 3.0 * cell_c) ** 2
    )
    smooth_b = 13.0 / 12.0 * (cell_b - 2.0 * cell_c + cell_d) ** 2 + 0.25 * (cell_b - cell_d) ** 2
    smooth_c = (
        13.0 / 12.0 * (cell_c - 2.0 * cell_d + cell_e) ** 2
        + 0.25 * (3.0 * cell_c - 4.0 * cell_d + cell_e) ** 2
    )
    weight_a = 0.1 / (WENO_EPS + smooth_a) ** 2
    weight_b = 0.6 / (WENO_EPS + smooth_b) ** 2
    weight_c = 0.3 / (WENO_EPS + smooth_c) ** 2
    guess_a = (2.0 * cell_a - 7.0 * cell_b + 11.0 * cell_c) / 6.0
    guess_b = (-cell_b + 5.0 * cell_c + 2.0 * cell_d) / 6.0
    guess_c = (2.0 * cell_c + 5.0 * cell_d - cell_e) / 6.0
    return (weight_a * guess_a + weight_b * guess_b + weight_c * guess_c) / (
        weight_a + weight_b + weight_c
    )


def divergence(fields, dim_index, normal_index, wave_speed):
    flux_all = face_flux(fields, normal_index)
    upwind = 0.5 * (flux_all + wave_speed * fields)
    downwind = 0.5 * (flux_all - wave_speed * fields)
    faces = fields.shape[dim_index] - 5

    def cell_run(source, start):
        return lax.slice_in_dim(source, start, start + faces, axis=dim_index)

    face_sum = weno_face(
        cell_run(upwind, 0),
        cell_run(upwind, 1),
        cell_run(upwind, 2),
        cell_run(upwind, 3),
        cell_run(upwind, 4),
    )
    face_sum = face_sum + weno_face(
        cell_run(downwind, 5),
        cell_run(downwind, 4),
        cell_run(downwind, 3),
        cell_run(downwind, 2),
        cell_run(downwind, 1),
    )
    upper = lax.slice_in_dim(face_sum, 1, faces, axis=dim_index)
    lower = lax.slice_in_dim(face_sum, 0, faces - 1, axis=dim_index)
    return lower - upper


def flux_rhs(fields, wave_speed):
    final_dim = fields.ndim - 1
    along_x = divergence(fields, final_dim - 1, 0, wave_speed)[..., 3:-3]
    along_y = divergence(fields, final_dim, 1, wave_speed)[..., 3:-3, :]
    center = fields[..., 3:-3, 3:-3]
    laplace = (
        fields[..., 4:-2, 3:-3]
        + fields[..., 2:-4, 3:-3]
        + fields[..., 3:-3, 4:-2]
        + fields[..., 3:-3, 2:-4]
        - 4.0 * center
    )
    momentum_mask = jnp.array([0.0, 1.0, 1.0, 1.0, 1.0], jnp.float32).reshape(
        (5,) + (1,) * (fields.ndim - 1)
    )
    return along_x + along_y + VISCOSITY * momentum_mask * laplace


def closure(fields, weight_in, bias_in, weight_out, bias_out):
    shape_tail = (1,) * (fields.ndim - 1)
    hidden = jnp.tanh(
        jnp.einsum("hf,f...->h...", weight_in, fields, precision=lax.Precision.HIGHEST)
        + bias_in.reshape((-1,) + shape_tail)
    )
    return fields[0] * (
        jnp.einsum("fh,h...->f...", weight_out, hidden, precision=lax.Precision.HIGHEST)
        + bias_out.reshape((-1,) + shape_tail)
    )


def section_local(state, cotangent, wave_speed, weight_in, bias_in, weight_out, bias_out):

    def flux_part(source):
        return flux_rhs(source, wave_speed)

    padded = padded_2(state, (("gx", 2), ("gy", 3)), 3)
    _, flux_back = jax.vjp(flux_part, padded)
    spread = flux_back(cotangent)[0]
    inner = spread[:, :, 3:-3, 3:-3]
    rows_x = inner.shape[2]
    rows_y = inner.shape[3]
    from_next_x = from_behind(spread[:, :, :3, 3:-3], "gx", -1)
    from_prev_x = from_behind(spread[:, :, -3:, 3:-3], "gx", 1)
    inner = inner + jnp.pad(from_prev_x, ((0, 0), (0, 0), (0, rows_x - 3), (0, 0)))
    inner = inner + jnp.pad(from_next_x, ((0, 0), (0, 0), (rows_x - 3, 0), (0, 0)))
    from_next_y = from_behind(spread[:, :, 3:-3, :3], "gy", -1)
    from_prev_y = from_behind(spread[:, :, 3:-3, -3:], "gy", 1)
    inner = inner + jnp.pad(from_prev_y, ((0, 0), (0, 0), (0, 0), (0, rows_y - 3)))
    inner = inner + jnp.pad(from_next_y, ((0, 0), (0, 0), (0, 0), (rows_y - 3, 0)))
    _, closure_back = jax.vjp(closure, state, weight_in, bias_in, weight_out, bias_out)
    pieces = closure_back(cotangent)
    return (inner + pieces[0], pieces[1:])


def reduce_section(grads):
    return lax.psum((grads[0], grads[1], grads[2], grads[3]), ("gx", "gy", "af"))


def shards(state_zero, state_one, cotangent, weight_in, bias_in, weight_out, bias_out):
    speed_zero, speed_one = lax.pmax(
        (max_speed(state_zero), max_speed(state_one)), ("gx", "gy", "af")
    )
    flux_one, grads_one = section_local(
        state_one, cotangent, speed_one, weight_in, bias_in, weight_out, bias_out
    )
    grad_middle = 0.25 * cotangent + 0.25 * TIME_STEP * flux_one
    flux_zero, grads_zero = section_local(
        state_zero, grad_middle, speed_zero, weight_in, bias_in, weight_out, bias_out
    )
    grad_state = 0.75 * cotangent + grad_middle + TIME_STEP * flux_zero
    cells_total = (
        state_zero.shape[1]
        * state_zero.shape[2]
        * state_zero.shape[3]
        * lax.axis_size("gx")
        * lax.axis_size("gy")
        * lax.axis_size("af")
    )
    scale = 1.0 / cells_total
    summed_one = reduce_section(grads_one)
    summed_zero = reduce_section(grads_zero)
    totals = jax.tree.map(
        lambda first, second: (0.25 * TIME_STEP * first + TIME_STEP * second) * scale,
        tuple(summed_one),
        tuple(summed_zero),
    )
    return (grad_state, totals[0], totals[1], totals[2], totals[3])


def solution(mesh):
    placed = (
        P(None, "af", ("cases", "gx"), "gy"),
        P(None, "af", ("cases", "gx"), "gy"),
        P(None, "af", ("cases", "gx"), "gy"),
        P(),
        P(),
        P(),
        P(),
    )
    return jax.shard_map(
        shards,
        mesh=mesh,
        in_specs=placed,
        out_specs=(
            P(None, "af", ("cases", "gx"), "gy"),
            P("cases", None),
            P("cases"),
            P("cases", None),
            P("cases"),
        ),
        check_vma=False,
    )
```

profile of v0, /device:TPU:0, one launch (start us, length us, event | category | flops | bytes accessed | tf_op | source)
XLA Modules:
  0.0 168.5 jit_solution(16587958447637736621)
XLA Ops:
  0.6 0.9 fusion.121
  1.5 3.1 %collective-permute-start = (f32[5,2,3,128]{3,0,2,1:T(8,128)S(1)}, f32[5,2,3,128]{3,0,2,1:T(8,128)S(1)}, u32[]{:S(2)}, u32[]{:S(2)}) collective-permute-start(f32[5,2,3,128]{3,0,2,1:T(8,128)S(1)} %copy.61), channel_id=1, source_target_pairs={{0,4},{4,8},{8,12},{12,0},{1,5},{5,9},{9,13},{13,1},{2,6},{6,10},{... | collective-permute-start | bytes 46088 | tf_op jit(solution)/shard_map/ppermute | solution.py:19
  4.6 2.1 %collective-permute-start.1 = (f32[5,2,3,128]{3,0,2,1:T(8,128)S(1)}, f32[5,2,3,128]{3,0,2,1:T(8,128)S(1)}, u32[]{:S(2)}, u32[]{:S(2)}) collective-permute-start(f32[5,2,3,128]{3,0,2,1:T(8,128)S(1)} %copy.62), channel_id=1, source_target_pairs={{4,0},{8,4},{12,8},{0,12},{5,1},{9,5},{13,9},{1,13},{6,2},{10,6},{... | collective-permute-start | bytes 46088 | tf_op jit(solution)/shard_map/ppermute | solution.py:21
  6.8 3.8 %collective-permute-start.9 = (f32[5,2,3,128]{3,0,2,1:T(8,128)S(1)}, f32[5,2,3,128]{3,0,2,1:T(8,128)S(1)}, u32[]{:S(2)}, u32[]{:S(2)}) collective-permute-start(f32[5,2,3,128]{3,0,2,1:T(8,128)S(1)} %copy.60), channel_id=1, source_target_pairs={{4,0},{8,4},{12,8},{0,12},{5,1},{9,5},{13,9},{1,13},{6,2},{10,6},{... | collective-permute-start | bytes 46088 | tf_op jit(solution)/shard_map/ppermute | solution.py:21
  16.1 1.1 convolution_bitcast_fusion.5
  17.3 1.3 fusion.124
  18.5 1.0 fusion.11
  20.2 30.1 %all-reduce.121 = (f32[]{:T(128)}, f32[]{:T(128)}) all-reduce(f32[]{:T(128)} %fusion.85, f32[]{:T(128)} %fusion.84), channel_id=1, replica_groups=mesh['cases'=2,'gx'=4,'gy'=2,'af'=2] {'gx','gy','af'}, use_global_device_ids=true, to_apply=%region_4.5 | all-reduce | flops 2 | bytes 16 | tf_op jit(solution)/shard_map/pmax | solution.py:169
  51.2 2.0 %collective-permute-start.3 = (f32[5,2,14,3]{3,0,2,1:T(8,128)S(1)}, f32[5,2,14,3]{3,0,2,1:T(8,128)S(1)}, u32[]{:S(2)}, u32[]{:S(2)}) collective-permute-start(f32[5,2,14,3]{3,0,2,1:T(8,128)S(1)} %get-tuple-element.337), channel_id=1, source_target_pairs={{2,0},{0,2},{3,1},{1,3},{6,4},{4,6},{7,5},{5,7},{10,8},{8,10},{11,... | collective-permute-start | bytes 5048 | tf_op jit(solution)/shard_map/ppermute | solution.py:21
  53.5 1.9 %collective-permute-start.11 = (f32[5,2,14,3]{3,0,2,1:T(8,128)S(1)}, f32[5,2,14,3]{3,0,2,1:T(8,128)S(1)}, u32[]{:S(2)}, u32[]{:S(2)}) collective-permute-start(f32[5,2,14,3]{3,0,2,1:T(8,128)S(1)} %get-tuple-element.339), channel_id=1, source_target_pairs={{2,0},{0,2},{3,1},{1,3},{6,4},{4,6},{7,5},{5,7},{10,8},{8,10},{11,... | collective-permute-start | bytes 5048 | tf_op jit(solution)/shard_map/ppermute | solution.py:21
  55.5 1.8 %collective-permute-done.2 = f32[5,2,14,3]{3,0,2,1:T(8,128)S(1)} collective-permute-done((f32[5,2,14,3]{3,0,2,1:T(8,128)S(1)}, f32[5,2,14,3]{3,0,2,1:T(8,128)S(1)}, u32[]{:S(2)}, u32[]{:S(2)}) %collective-permute-start.2) | collective-permute-done | bytes 1712 | tf_op jit(solution)/shard_map/ppermute | solution.py:19
  57.2 2.5 %collective-permute-done.3 = f32[5,2,14,3]{3,0,2,1:T(8,128)S(1)} collective-permute-done((f32[5,2,14,3]{3,0,2,1:T(8,128)S(1)}, f32[5,2,14,3]{3,0,2,1:T(8,128)S(1)}, u32[]{:S(2)}, u32[]{:S(2)}) %collective-permute-start.3) | collective-permute-done | bytes 1712 | tf_op jit(solution)/shard_map/ppermute | solution.py:21
  60.7 1.5 collective-permute-done.10
  62.2 1.3 collective-permute-done.11
  66.2 1.5 subtract_multiply_fusion
  67.7 1.7 add_add_fusion.39
  78.0 1.5 add_add_fusion.6
  80.0 1.7 %collective-permute-start.7 = (f32[5,2,8,3]{3,0,2,1:T(8,128)S(1)}, f32[5,2,8,3]{3,0,2,1:T(8,128)S(1)}, u32[]{:S(2)}, u32[]{:S(2)}) collective-permute-start(f32[5,2,8,3]{3,0,2,1:T(8,128)S(1)} %get-tuple-element.315), channel_id=1, source_target_pairs={{0,2},{2,0},{1,3},{3,1},{4,6},{6,4},{5,7},{7,5},{8,10},{10,8},{9,1... | collective-permute-start | bytes 2888 | tf_op jit(solution)/shard_map/ppermute | solution.py:30
  81.8 3.8 %collective-permute-start.5 = (f32[5,2,3,128]{3,0,2,1:T(8,128)S(1)}, f32[5,2,3,128]{3,0,2,1:T(8,128)S(1)}, u32[]{:S(2)}, u32[]{:S(2)}) collective-permute-start(f32[5,2,3,128]{3,0,2,1:T(8,128)S(1)} %get-tuple-element.313), channel_id=1, source_target_pairs={{0,12},{4,0},{8,4},{12,8},{1,13},{5,1},{9,5},{13,9},{2,14},{6,2},{... | collective-permute-start | bytes 46088 | tf_op jit(solution)/shard_map/ppermute | solution.py:30
  89.4 1.6 add_add_fusion.23
  98.3 1.5 add_add_fusion
  100.9 1.7 %collective-permute-start.15 = (f32[5,2,8,3]{3,0,2,1:T(8,128)S(1)}, f32[5,2,8,3]{3,0,2,1:T(8,128)S(1)}, u32[]{:S(2)}, u32[]{:S(2)}) collective-permute-start(f32[5,2,8,3]{3,0,2,1:T(8,128)S(1)} %get-tuple-element.291), channel_id=1, source_target_pairs={{0,2},{2,0},{1,3},{3,1},{4,6},{6,4},{5,7},{7,5},{8,10},{10,8},{9,1... | collective-permute-start | bytes 2888 | tf_op jit(solution)/shard_map/ppermute | solution.py:30
  102.6 3.8 %collective-permute-start.13 = (f32[5,2,3,128]{3,0,2,1:T(8,128)S(1)}, f32[5,2,3,128]{3,0,2,1:T(8,128)S(1)}, u32[]{:S(2)}, u32[]{:S(2)}) collective-permute-start(f32[5,2,3,128]{3,0,2,1:T(8,128)S(1)} %get-tuple-element.289), channel_id=1, source_target_pairs={{0,12},{4,0},{8,4},{12,8},{1,13},{5,1},{9,5},{13,9},{2,14},{6,2},{... | collective-permute-start | bytes 46088 | tf_op jit(solution)/shard_map/ppermute | solution.py:30
  107.1 57.7 %all-reduce.120 = (f32[64,5]{0,1:T(8,128)S(1)}, f32[64,5]{0,1:T(8,128)S(1)}, f32[64]{0:T(128)S(1)}, f32[64]{0:T(128)S(1)}, f32[5,64]{1,0:T(8,128)S(1)}, /*index=...) all-reduce(f32[64,5]{0,1:T(8,128)S(1)} %convolution_bitcast_fusion., ...), channel_id=1, replica_groups=mesh['cases'=2,'gx'=4,'gy'=2,'af'=2] {'gx','gy','af'}, use_global_device_ids=true, to_apply=%region_7.8 | all-reduce | flops 1418 | bytes 11344 | tf_op jit(solution)/shard_map/psum | solution.py:165
  (168 shorter events, 35.0 us)
Async XLA Ops:
  0.6 11.9 %copy-start = (f32[64,5]{0,1:T(8,128)S(1)}, f32[64,5]{0,1:T(8,128)}, u32[]{:S(2)}) copy-start(f32[64,5]{0,1:T(8,128)} %param.12) | copy-start | bytes 3844
  1.5 5.2 %copy-start.3 = (f32[5,2,8,128]{3,2,1,0:T(8,128)S(1)}, f32[5,2,8,128]{3,2,1,0:T(8,128)}, u32[]{:S(2)}) copy-start(f32[5,2,8,128]{3,2,1,0:T(8,128)} %param.9) | copy-start | bytes 122884
  1.5 49.5 %collective-permute-start = (f32[5,2,3,128]{3,0,2,1:T(8,128)S(1)}, f32[5,2,3,128]{3,0,2,1:T(8,128)S(1)}, u32[]{:S(2)}, u32[]{:S(2)}) collective-permute-start(f32[5,2,3,128]{3,0,2,1:T(8,128)S(1)} %copy.61), channel_id=1, source_target_pairs={{0,4},{4,8},{8,12},{12,0},{1,5},{5,9},{9,13},{13,1},{2,6},{6,10},{... | collective-permute-start | bytes 46088 | tf_op jit(solution)/shard_map/ppermute | solution.py:19
  4.6 46.4 %collective-permute-start.1 = (f32[5,2,3,128]{3,0,2,1:T(8,128)S(1)}, f32[5,2,3,128]{3,0,2,1:T(8,128)S(1)}, u32[]{:S(2)}, u32[]{:S(2)}) collective-permute-start(f32[5,2,3,128]{3,0,2,1:T(8,128)S(1)} %copy.62), channel_id=1, source_target_pairs={{4,0},{8,4},{12,8},{0,12},{5,1},{9,5},{13,9},{1,13},{6,2},{10,6},{... | collective-permute-start | bytes 46088 | tf_op jit(solution)/shard_map/ppermute | solution.py:21
  6.7 3.9 %copy-start.2 = (f32[5,2,8,128]{3,2,1,0:T(8,128)S(1)}, f32[5,2,8,128]{3,2,1,0:T(8,128)}, u32[]{:S(2)}) copy-start(f32[5,2,8,128]{3,2,1,0:T(8,128)} %param.10) | copy-start | bytes 122884
  6.8 46.5 %collective-permute-start.8 = (f32[5,2,3,128]{3,0,2,1:T(8,128)S(1)}, f32[5,2,3,128]{3,0,2,1:T(8,128)S(1)}, u32[]{:S(2)}, u32[]{:S(2)}) collective-permute-start(f32[5,2,3,128]{3,0,2,1:T(8,128)S(1)} %copy.59), channel_id=1, source_target_pairs={{0,4},{4,8},{8,12},{12,0},{1,5},{5,9},{9,13},{13,1},{2,6},{6,10},{... | collective-permute-start | bytes 46088 | tf_op jit(solution)/shard_map/ppermute | solution.py:19
  6.8 46.4 %collective-permute-start.9 = (f32[5,2,3,128]{3,0,2,1:T(8,128)S(1)}, f32[5,2,3,128]{3,0,2,1:T(8,128)S(1)}, u32[]{:S(2)}, u32[]{:S(2)}) collective-permute-start(f32[5,2,3,128]{3,0,2,1:T(8,128)S(1)} %copy.60), channel_id=1, source_target_pairs={{4,0},{8,4},{12,8},{0,12},{5,1},{9,5},{13,9},{1,13},{6,2},{10,6},{... | collective-permute-start | bytes 46088 | tf_op jit(solution)/shard_map/ppermute | solution.py:21
  51.2 6.1 %collective-permute-start.2 = (f32[5,2,14,3]{3,0,2,1:T(8,128)S(1)}, f32[5,2,14,3]{3,0,2,1:T(8,128)S(1)}, u32[]{:S(2)}, u32[]{:S(2)}) collective-permute-start(f32[5,2,14,3]{3,0,2,1:T(8,128)S(1)} %get-tuple-element.336), channel_id=1, source_target_pairs={{0,2},{2,0},{1,3},{3,1},{4,6},{6,4},{5,7},{7,5},{8,10},{10,8},{9,1... | collective-permute-start | bytes 5048 | tf_op jit(solution)/shard_map/ppermute | solution.py:19
  51.2 8.5 %collective-permute-start.3 = (f32[5,2,14,3]{3,0,2,1:T(8,128)S(1)}, f32[5,2,14,3]{3,0,2,1:T(8,128)S(1)}, u32[]{:S(2)}, u32[]{:S(2)}) collective-permute-start(f32[5,2,14,3]{3,0,2,1:T(8,128)S(1)} %get-tuple-element.337), channel_id=1, source_target_pairs={{2,0},{0,2},{3,1},{1,3},{6,4},{4,6},{7,5},{5,7},{10,8},{8,10},{11,... | collective-permute-start | bytes 5048 | tf_op jit(solution)/shard_map/ppermute | solution.py:21
  53.4 8.8 %collective-permute-start.10 = (f32[5,2,14,3]{3,0,2,1:T(8,128)S(1)}, f32[5,2,14,3]{3,0,2,1:T(8,128)S(1)}, u32[]{:S(2)}, u32[]{:S(2)}) collective-permute-start(f32[5,2,14,3]{3,0,2,1:T(8,128)S(1)} %get-tuple-element.338), channel_id=1, source_target_pairs={{0,2},{2,0},{1,3},{3,1},{4,6},{6,4},{5,7},{7,5},{8,10},{10,8},{9,1... | collective-permute-start | bytes 5048 | tf_op jit(solution)/shard_map/ppermute | solution.py:19
  53.5 10.0 %collective-permute-start.11 = (f32[5,2,14,3]{3,0,2,1:T(8,128)S(1)}, f32[5,2,14,3]{3,0,2,1:T(8,128)S(1)}, u32[]{:S(2)}, u32[]{:S(2)}) collective-permute-start(f32[5,2,14,3]{3,0,2,1:T(8,128)S(1)} %get-tuple-element.339), channel_id=1, source_target_pairs={{2,0},{0,2},{3,1},{1,3},{6,4},{4,6},{7,5},{5,7},{10,8},{8,10},{11,... | collective-permute-start | bytes 5048 | tf_op jit(solution)/shard_map/ppermute | solution.py:21
  60.6 3.9 %copy-start.14 = (f32[1,2,14,134]{3,0,2,1:T(1,128)}, f32[1,2,14,134]{3,0,2,1:T(1,128)S(1)}, u32[]{:S(2)}) copy-start(f32[1,2,14,134]{3,0,2,1:T(1,128)S(1)} %get-tuple-element.151) | copy-start | bytes 45028
  60.7 3.8 %copy-start.18 = (f32[1,2,14,134]{3,0,2,1:T(1,128)}, f32[1,2,14,134]{3,0,2,1:T(1,128)S(1)}, u32[]{:S(2)}) copy-start(f32[1,2,14,134]{3,0,2,1:T(1,128)S(1)} %get-tuple-element.197) | copy-start | bytes 45028
  79.7 7.8 %copy-start.20 = (f32[2,8,128]{2,1,0:T(8,128)S(1)}, f32[2,8,128]{2,1,0:T(8,128)}, u32[]{:S(2)}) copy-start(f32[2,8,128]{2,1,0:T(8,128)} %slice_bitcast_fusion) | copy-start | bytes 24580
  79.8 7.1 %collective-permute-start.6 = (f32[5,2,8,3]{3,0,2,1:T(8,128)S(1)}, f32[5,2,8,3]{3,0,2,1:T(8,128)S(1)}, u32[]{:S(2)}, u32[]{:S(2)}) collective-permute-start(f32[5,2,8,3]{3,0,2,1:T(8,128)S(1)} %get-tuple-element.314), channel_id=1, source_target_pairs={{0,2},{2,0},{1,3},{3,1},{4,6},{6,4},{5,7},{7,5},{8,10},{10,8},{9,1... | collective-permute-start | bytes 2888 | tf_op jit(solution)/shard_map/ppermute | solution.py:30
  80.0 6.8 %collective-permute-start.7 = (f32[5,2,8,3]{3,0,2,1:T(8,128)S(1)}, f32[5,2,8,3]{3,0,2,1:T(8,128)S(1)}, u32[]{:S(2)}, u32[]{:S(2)}) collective-permute-start(f32[5,2,8,3]{3,0,2,1:T(8,128)S(1)} %get-tuple-element.315), channel_id=1, source_target_pairs={{0,2},{2,0},{1,3},{3,1},{4,6},{6,4},{5,7},{7,5},{8,10},{10,8},{9,1... | collective-permute-start | bytes 2888 | tf_op jit(solution)/shard_map/ppermute | solution.py:30
  81.8 5.6 %collective-permute-start.4 = (f32[5,2,3,128]{3,0,2,1:T(8,128)S(1)}, f32[5,2,3,128]{3,0,2,1:T(8,128)S(1)}, u32[]{:S(2)}, u32[]{:S(2)}) collective-permute-start(f32[5,2,3,128]{3,0,2,1:T(8,128)S(1)} %get-tuple-element.312), channel_id=1, source_target_pairs={{0,4},{4,8},{8,12},{12,0},{1,5},{5,9},{9,13},{13,1},{2,6},{6,10},{... | collective-permute-start | bytes 46088 | tf_op jit(solution)/shard_map/ppermute | solution.py:30
  81.8 5.6 %collective-permute-start.5 = (f32[5,2,3,128]{3,0,2,1:T(8,128)S(1)}, f32[5,2,3,128]{3,0,2,1:T(8,128)S(1)}, u32[]{:S(2)}, u32[]{:S(2)}) collective-permute-start(f32[5,2,3,128]{3,0,2,1:T(8,128)S(1)} %get-tuple-element.313), channel_id=1, source_target_pairs={{0,12},{4,0},{8,4},{12,8},{1,13},{5,1},{9,5},{13,9},{2,14},{6,2},{... | collective-permute-start | bytes 46088 | tf_op jit(solution)/shard_map/ppermute | solution.py:30
  85.6 1.8 %copy-start.22 = (f32[2,8,128]{2,1,0:T(8,128)S(1)}, f32[2,8,128]{2,1,0:T(8,128)}, u32[]{:S(2)}) copy-start(f32[2,8,128]{2,1,0:T(8,128)} %fusion.11) | copy-start | bytes 24580
  100.5 66.9 %collective-permute-start.14 = (f32[5,2,8,3]{3,0,2,1:T(8,128)S(1)}, f32[5,2,8,3]{3,0,2,1:T(8,128)S(1)}, u32[]{:S(2)}, u32[]{:S(2)}) collective-permute-start(f32[5,2,8,3]{3,0,2,1:T(8,128)S(1)} %get-tuple-element.290), channel_id=1, source_target_pairs={{0,2},{2,0},{1,3},{3,1},{4,6},{6,4},{5,7},{7,5},{8,10},{10,8},{9,1... | collective-permute-start | bytes 2888 | tf_op jit(solution)/shard_map/ppermute | solution.py:30
  100.9 66.6 %collective-permute-start.15 = (f32[5,2,8,3]{3,0,2,1:T(8,128)S(1)}, f32[5,2,8,3]{3,0,2,1:T(8,128)S(1)}, u32[]{:S(2)}, u32[]{:S(2)}) collective-permute-start(f32[5,2,8,3]{3,0,2,1:T(8,128)S(1)} %get-tuple-element.291), channel_id=1, source_target_pairs={{0,2},{2,0},{1,3},{3,1},{4,6},{6,4},{5,7},{7,5},{8,10},{10,8},{9,1... | collective-permute-start | bytes 2888 | tf_op jit(solution)/shard_map/ppermute | solution.py:30
  102.6 64.9 %collective-permute-start.12 = (f32[5,2,3,128]{3,0,2,1:T(8,128)S(1)}, f32[5,2,3,128]{3,0,2,1:T(8,128)S(1)}, u32[]{:S(2)}, u32[]{:S(2)}) collective-permute-start(f32[5,2,3,128]{3,0,2,1:T(8,128)S(1)} %get-tuple-element.288), channel_id=1, source_target_pairs={{0,4},{4,8},{8,12},{12,0},{1,5},{5,9},{9,13},{13,1},{2,6},{6,10},{... | collective-permute-start | bytes 46088 | tf_op jit(solution)/shard_map/ppermute | solution.py:30
  102.6 3.8 %copy-start.23 = (f32[5,64]{1,0:T(8,128)S(1)}, f32[5,64]{1,0:T(8,128)}, u32[]{:S(2)}) copy-start(f32[5,64]{1,0:T(8,128)} %convolution_bitcast_fusion.5) | copy-start | bytes 3844
  102.6 64.9 %collective-permute-start.13 = (f32[5,2,3,128]{3,0,2,1:T(8,128)S(1)}, f32[5,2,3,128]{3,0,2,1:T(8,128)S(1)}, u32[]{:S(2)}, u32[]{:S(2)}) collective-permute-start(f32[5,2,3,128]{3,0,2,1:T(8,128)S(1)} %get-tuple-element.289), channel_id=1, source_target_pairs={{0,12},{4,0},{8,4},{12,8},{1,13},{5,1},{9,5},{13,9},{2,14},{6,2},{... | collective-permute-start | bytes 46088 | tf_op jit(solution)/shard_map/ppermute | solution.py:30
  (23 other events, 19.6 us)
where the time goes:
time: 169 us
  blocking collectives  87.8 us (52%)
  other arithmetic  29.1 us (17%)
  starting transfers between devices  24.9 us (15%)
  matrix products  8.27 us (5%)
  local copies, waits for them, and re-layouts  8.23 us (5%)
  waiting for transfers between devices  7.65 us (5%)
  between operations  2.6 us (2%)
    psum x1, blocking collectives, reduce_section(): lax.psum((grads[0], grads[1], grads[2], grads[3]), ('gx', 'gy', 'af'))  57.7 us
    pmax x1, blocking collectives, shards(): lax.pmax((max_speed(state_zero), max_speed(state_one)), ('gx', 'gy', 'af'))  30.1 us
    ppermute x8, starting transfers between devices, from_behind(): lax.ppermute(array, axis, [(i, (i + by) % count) for i in range(count)])  11.7 us
    ppermute x4, starting transfers between devices, padded_2(): lax.ppermute(head, axis, [((i + 1) % count, i) for i in range(count)])  9.86 us
    unnamed x71, local copies, waits for them, and re-layouts  5.4 us
    add_any x6, other arithmetic, weno_face(): cell_c - 2.0 * cell_d + cell_e  5.06 us
    dot_general x6, matrix products, closure(): jnp.einsum('fh,h...->f...', weight_out, hidden, precision=lax.Precision.H...  5.04 us
    add_any x8, other arithmetic, weno_face(): cell_a - 2.0 * cell_b + cell_c  3.97 us
  transfers between devices with their start and end apart: 16, of which 5 were waited for; matrix products, arithmetic and copies ran while one was open for 8% of the time, Pallas kernels for 0%

commit v1 on v0

v1 whole, which is shorter than its diff:
```python
import functools

import jax
import jax.numpy as jnp
from jax import lax
from jax.experimental import pallas as pl
from jax.experimental.pallas import tpu as pltpu
from jax.sharding import PartitionSpec as P

MESH = pl.DeviceIdType.MESH
GAMMA = 1.4
TIME_STEP = 0.1
VISCOSITY = 0.2
WENO_EPS = 1e-06
F32 = jnp.float32
BF16 = jnp.bfloat16


def shifted(x, by, axis):
    return pltpu.roll(x, (-by) % x.shape[axis], axis)


def high_low(x):
    high = x.astype(BF16).astype(F32)
    return high, x - high


def weno_grads(d0, d1, d2, d3, w):
    a0 = 8.0 * d0 - 11.0 * d1
    a1 = 20.0 * d1 - 11.0 * d0
    b0 = 8.0 * d1 - 5.0 * d2
    b1 = 8.0 * d2 - 5.0 * d1
    c0 = 20.0 * d2 - 11.0 * d3
    c1 = 8.0 * d3 - 11.0 * d2
    eps = 6.0 * WENO_EPS
    ra = 1.0 / (eps + d0 * a0 + d1 * a1)
    rb = 1.0 / (eps + d1 * b0 + d2 * b1)
    rc = 1.0 / (eps + d2 * c0 + d3 * c1)
    wa = ra * ra
    wb = 6.0 * (rb * rb)
    wc = 3.0 * (rc * rc)
    ga = 5.0 * d1 - 2.0 * d0
    gb = d1 + 2.0 * d2
    gc = 4.0 * d2 - d3
    inv = 1.0 / (wa + wb + wc)
    mean = (wa * ga + wb * gb + wc * gc) * inv
    scale = w * inv
    ka = wa * scale
    kb = wb * scale
    kc = wc * scale
    ma = 4.0 * ka * ra * (mean - ga)
    mb = 4.0 * kb * rb * (mean - gb)
    mc = 4.0 * kc * rc * (mean - gc)
    return (
        ma * a0 - 2.0 * ka,
        ma * a1 + 5.0 * ka + mb * b0 + kb,
        mb * b1 + 2.0 * kb + mc * c0 + 4.0 * kc,
        mc * c1 - kc,
    )


def line_adjoint(up, down, v, axis, own):
    sh = functools.partial(shifted, axis=axis)
    w = sh(v, 1) - v
    w6 = w * (1.0 / 6.0)
    d = sh(up, 1) - up
    g = weno_grads(sh(d, -2), sh(d, -1), d, sh(d, 1), w6)
    gp = sh(g[0], 2) + sh(g[1], 1) + g[2] + sh(g[3], -1)
    d = down - sh(down, 1)
    g = weno_grads(sh(d, 2), sh(d, 1), d, sh(d, -1), w6)
    gm = sh(g[0], -2) + sh(g[1], -1) + g[2] + sh(g[3], 1)
    wb = sh(w, -1)
    t = gp - gm
    s = gp + gm
    total = w + wb + sh(t, -1) - t
    apart = w - wb + sh(s, -1) - s
    laplace = sh(v, 1) + sh(v, -1) - 2.0 * v
    return own(total), own(apart), own(laplace)


def flux_parts(q, k):
    inv = 1.0 / q[0]
    pressure = (GAMMA - 1.0) * (
        q[4] - 0.5 * (q[1] * q[1] + q[2] * q[2] + q[3] * q[3]) * inv
    )
    u = q[k + 1] * inv
    f = [q[k + 1], q[1] * u, q[2] * u, q[3] * u, (q[4] + pressure) * u]
    f[k + 1] = f[k + 1] + pressure
    return f


def kernel(
    sizes,
    s0_ref, s1_ref, ct_ref, win_ref, bin_ref, wout_ref, bout_ref,
    out_ref, gwin_ref, gbin_ref, gwout_ref, gbout_ref,
    q0p, q1p, ctp, gmp, cqp, wtile, w1, w2, w3, bcol,
    fxp, fxm, fyp, fym, vx, vy, gx_s, gy_s, gq_s,
    xs, xr, ys, yr, spd, prm,
    xsend, xrecv, ysend, yrecv, gsend, grecv, psend, precv,
):
    GX, GY, AF = sizes
    ix, iy, ia = lax.axis_index("gx"), lax.axis_index("gy"), lax.axis_index("af")
    ic = lax.axis_index("cases")
    joint = GX * GY * AF <= 16
    if joint:
        stages = [[(a, b, c) for a in range(GX) for b in range(GY) for c in range(AF)]]
    else:
        stages = [
            [(a, 0, 0) for a in range(GX)],
            [(0, b, 0) for b in range(GY)],
            [(0, 0, c) for c in range(AF)],
        ]

    def place(off):
        return (
            ic,
            lax.rem(ix + off[0], GX) if off[0] else ix,
            lax.rem(iy + off[1], GY) if off[1] else iy,
            lax.rem(ia + off[2], AF) if off[2] else ia,
        )

    barrier = pltpu.get_barrier_semaphore()
    greeted = 0
    for stage in stages:
        for off in stage[1:]:
            pl.semaphore_signal(barrier, inc=1, device_id=place(off), device_id_type=MESH)
            greeted += 1

    row = lax.broadcasted_iota(jnp.int32, (8, 128), 0)
    lane = lax.broadcasted_iota(jnp.int32, (8, 128), 1)
    upper = row < 4

    ones = jnp.ones((16, 128), F32)
    for ref, src in ((q0p, s0_ref), (q1p, s1_ref), (ctp, ct_ref)):
        ref[0:80, :] = src[...]
    for ref in (q0p, q1p):
        ref[80:96, :] = ones
        ref[96:128, :] = jnp.zeros((32, 128), F32)
    for ref in (ctp, gmp):
        ref[80:128, :] = jnp.zeros((48, 128), F32)

    def tile(ref, f, z):
        return ref[f * 16 + z * 8 : f * 16 + z * 8 + 8, :]

    def pack(ref, base, yslot):
        packed = jnp.zeros((8, 128), F32)
        for f in range(5):
            one, two = tile(ref, f, 0), pltpu.roll(tile(ref, f, 1), 4, 0)
            xs[0, base + f] = jnp.where(upper, one, two)
            xs[1, base + f] = jnp.where(upper, two, one)
            for z in range(2):
                t = f * 2 + z
                moved = pltpu.roll(tile(ref, f, z), (4 + 8 * t) % 128, 1)
                packed = jnp.where((lane >= 8 * t) & (lane < 8 * t + 8), moved, packed)
        ys[yslot] = packed

    def x_copies(base, count, sem):
        made = []
        for way in range(2):
            off = (GX - 1, 0, 0) if way == 0 else (1, 0, 0)
            made.append(
                pltpu.make_async_remote_copy(
                    src_ref=xs.at[way, pl.ds(base, count)],
                    dst_ref=xr.at[way, pl.ds(base, count)],
                    send_sem=xsend.at[way, sem],
                    recv_sem=xrecv.at[way, sem],
                    device_id=place(off),
                    device_id_type=MESH,
                )
            )
        return made

    def y_copies(base, count, sem):
        made = []
        for way in range(1 if GY == 2 else 2):
            off = (0, 1, 0) if way == 0 else (0, GY - 1, 0)
            made.append(
                pltpu.make_async_remote_copy(
                    src_ref=ys.at[pl.ds(base, count)],
                    dst_ref=yr.at[way, pl.ds(base, count)],
                    send_sem=ysend.at[way, sem],
                    recv_sem=yrecv.at[way, sem],
                    device_id=place(off),
                    device_id_type=MESH,
                )
            )
        return made

    def x_halo(base, f):
        ahead, behind = xr[0, base + f], xr[1, base + f]
        return (
            jnp.where(upper, ahead, behind),
            pltpu.roll(jnp.where(upper, behind, ahead), 4, 0),
        )

    def y_packed(slot):
        if GY == 2:
            return yr[0, slot]
        return jnp.where(lax.rem(lane, 8) < 4, yr[0, slot], yr[1, slot])

    def y_halo(packed, f, z):
        return pltpu.roll(packed, (-(4 + 8 * (f * 2 + z))) % 128, 1)

    pack(q1p, 0, 0)
    pack(ctp, 5, 1)
    pack(q0p, 10, 2)

    def top_speed(ref):
        best = None
        for z in range(2):
            q = [tile(ref, f, z) for f in range(5)]
            inv = 1.0 / q[0]
            pressure = (GAMMA - 1.0) * (
                q[4] - 0.5 * (q[1] * q[1] + q[2] * q[2] + q[3] * q[3]) * inv
            )
            sound = jnp.sqrt(GAMMA * pressure * inv)
            value = jnp.maximum(jnp.abs(q[1] * inv), jnp.abs(q[2] * inv)) + sound
            best = value if best is None else jnp.maximum(best, value)
        best = jnp.max(best, axis=0, keepdims=True)
        return jnp.broadcast_to(jnp.max(best, axis=1, keepdims=True), (1, 128))

    fastest = jnp.concatenate([top_speed(q0p), top_speed(q1p)], axis=1)

    wtile[...] = jnp.zeros_like(wtile)
    wtile[0:64, 0:5] = win_ref[...]
    wint = jnp.transpose(wtile[...])[0:8, :]
    wtile[0:8, :] = jnp.zeros((8, 128), F32)
    wtile[0:5, 0:64] = wout_ref[...]
    wout8 = wtile[0:8, :]
    wtile[0:8, :] = jnp.zeros((8, 128), F32)
    wtile[0:1, 0:64] = bin_ref[...]
    wtile[1:2, 0:5] = bout_ref[...]
    bin_row = wtile[0:1, :]
    bout_row = wtile[1:2, :]
    aug = jnp.where(row == 5, bin_row, wint)
    zero8 = jnp.zeros((8, 128), F32)
    ah, al = high_low(aug)
    oh, ol = high_low(wout8)
    fill = jnp.zeros((96, 128), F32)
    w1[...] = jnp.transpose(jnp.concatenate([ah, ah, al, zero8, fill], axis=0))[0:64, 0:32].astype(BF16)
    w2[...] = jnp.transpose(jnp.concatenate([oh, oh, ol, zero8, fill], axis=0))[0:64, 0:32].astype(BF16)
    ih, il = high_low(wint)
    lo_lane = lane < 64
    first = jnp.where(lo_lane, ih, pltpu.roll(ih, 64, 1))
    w3[:, 0:128] = jnp.concatenate([first, zero8], axis=0).astype(BF16)
    w3[:, 128:256] = jnp.concatenate([jnp.where(lo_lane, il, 0.0), zero8], axis=0).astype(BF16)
    bcol[...] = jnp.broadcast_to(
        jnp.sum(jnp.where(lane == row, jnp.broadcast_to(bout_row, (8, 128)), 0.0), axis=1, keepdims=True),
        (8, 128),
    )

    pl.semaphore_wait(barrier, greeted)

    a_copies = x_copies(0, 10, 0) + y_copies(0, 2, 0)
    b_copies = x_copies(10, 5, 1) + y_copies(2, 1, 1)
    c_copies = x_copies(15, 5, 2) + y_copies(3, 1, 2)

    def numbers(stage_index):
        base = sum(len(stages[s]) for s in range(stage_index))
        return [base + k for k in range(len(stages[stage_index]))]

    def my_rank(stage_index):
        if joint:
            return (ix * GY + iy) * AF + ia
        return (ix, iy, ia)[stage_index]

    def group_copies(buf, send, recv, stage_index):
        base = numbers(stage_index)[0]
        rank = base + my_rank(stage_index)
        made = []
        for k, off in enumerate(stages[stage_index]):
            if k == 0:
                continue
            made.append(
                pltpu.make_async_remote_copy(
                    src_ref=buf.at[rank],
                    dst_ref=buf.at[rank],
                    send_sem=send.at[base + k],
                    recv_sem=recv.at[base + k],
                    device_id=place(off),
                    device_id_type=MESH,
                )
            )
        return made

    started = []

    def start(copies):
        for c in copies:
            c.start()
            started.append(c)

    def begin_stage(buf, send, recv, s, value):
        buf[numbers(s)[0] + my_rank(s)] = value
        copies = group_copies(buf, send, recv, s)
        start(copies)
        return copies

    def end_stage(buf, s, copies, op):
        for c in copies:
            c.wait_recv()
        total = None
        for n in numbers(s):
            total = buf[n] if total is None else op(total, buf[n])
        return total

    spd_copies = begin_stage(spd, gsend, grecv, 0, fastest)
    start(a_copies)
    start(b_copies)

    def closure_back(qp, cp):
        acc = jnp.zeros((32, 256), F32)
        dsum = jnp.zeros((8, 256), F32)
        bb = jnp.concatenate([bcol[...], bcol[...]], axis=1)
        for chunk in range(8):
            r = 2 * chunk
            q8 = jnp.concatenate([qp[pl.ds(r, 8, stride=16), :], qp[pl.ds(r + 1, 8, stride=16), :]], axis=1)
            c8 = jnp.concatenate([cp[pl.ds(r, 8, stride=16), :], cp[pl.ds(r + 1, 8, stride=16), :]], axis=1)
            zero = jnp.zeros((8, 256), F32)
            qh, ql = high_low(q8)
            ch, cl = high_low(c8)
            pre = jnp.dot(w1[...], jnp.concatenate([qh, ql, qh, zero], axis=0).astype(BF16), preferred_element_type=F32)
            g = jnp.dot(w2[...], jnp.concatenate([ch, cl, ch, zero], axis=0).astype(BF16), preferred_element_type=F32)
            h = jnp.tanh(pre)
            t = g * (1.0 - h * h)
            hg = bb * c8
            prod = h * g
            for k in range(8):
                hg = hg + prod[8 * k : 8 * k + 8, :]
            hg = jnp.sum(hg, axis=0, keepdims=True)
            th, tl = high_low(t)
            hh, hl = high_low(h)
            thb, tlb = th.astype(BF16), tl.astype(BF16)
            hhb, hlb = hh.astype(BF16), hl.astype(BF16)
            stack = jnp.concatenate([thb, tlb, thb, jnp.zeros((64, 256), BF16)], axis=0)
            dq = jnp.dot(w3[...], stack, preferred_element_type=F32)[0:8, :]
            dens = q8[0:1, :]
            row2 = lax.broadcasted_iota(jnp.int32, (8, 256), 0)
            dq = dens * dq + jnp.where(row2 == 0, hg, 0.0)
            cqp[pl.ds(r, 8, stride=16), :] = dq[:, 0:128]
            cqp[pl.ds(r + 1, 8, stride=16), :] = dq[:, 128:256]
            pq = dens * q8
            dout = dens * c8
            dsum = dsum + dout
            ph, pw = high_low(pq)
            dh, dl = high_low(dout)
            left = jnp.concatenate([ph, pw, dh, dl], axis=0).astype(BF16)
            right = jnp.concatenate([thb, tlb, hhb, hlb], axis=0)
            acc = acc + lax.dot_general(left, right, (((1,), (1,)), ((), ())), preferred_element_type=F32)
        a = acc[0:8, 0:128]
        a = a + pltpu.roll(a, 64, 1) + acc[8:16, 0:128]
        b = acc[16:24, 128:256]
        b = b + pltpu.roll(b, 64, 1) + acc[24:32, 128:256]
        total = jnp.where(lane < 64, a, pltpu.roll(b, 64, 1))
        d = jnp.sum(dsum[:, 0:128] + dsum[:, 128:256], axis=1, keepdims=True)
        d = jnp.sum(jnp.where(lane == row, d, 0.0), axis=0, keepdims=True)
        return jnp.where(row == 6, d, total)

    def flux_back(qp, cp, xq, xc, yq, yc, speed, after):
        speed8 = jnp.broadcast_to(speed, (8, 128))
        speed16 = jnp.broadcast_to(speed, (16, 128))
        speed256 = jnp.concatenate([speed8, speed8], axis=1)
        hx = [x_halo(xq, f) for f in range(5)]
        cx = [x_halo(xc, f) for f in range(5)]
        pq, pc = y_packed(yq), y_packed(yc)
        for z in range(2):
            own = [tile(qp, f, z) for f in range(5)]
            q = [jnp.concatenate([own[f], hx[f][z]], axis=0) for f in range(5)]
            for f, part in enumerate(flux_parts(q, 0)):
                lead = speed16 * q[f]
                fxp[2 * f + z] = 0.5 * (part + lead)
                fxm[2 * f + z] = 0.5 * (part - lead)
            q = [jnp.concatenate([own[f], y_halo(pq, f, z)], axis=1) for f in range(5)]
            for f, part in enumerate(flux_parts(q, 1)):
                lead = speed256 * q[f]
                fyp[2 * f + z] = 0.5 * (part + lead)
                fym[2 * f + z] = 0.5 * (part - lead)
            for f in range(5):
                t = 2 * f + z
                v = tile(cp, f, z)
                vx[t, 0:8, :] = v
                vx[t, 8:16, :] = cx[f][z]
                vy[t, :, 0:128] = v
                vy[t, :, 128:256] = y_halo(pc, f, z)

        def body(t, _):
            total, apart, laplace = line_adjoint(fxp[t], fxm[t], vx[t], 0, lambda x: x[0:8, :])
            gx_s[t] = 0.5 * total
            total_y, apart_y, laplace_y = line_adjoint(fyp[t], fym[t], vy[t], 1, lambda x: x[:, 0:128])
            gy_s[t] = 0.5 * total_y
            viscous = jnp.where(t < 2, 0.0, VISCOSITY).astype(F32)
            gq_s[t] = 0.5 * speed8 * (apart + apart_y) + viscous * (laplace + laplace_y)
            return 0

        lax.fori_loop(0, 10, body, 0)

        for z in range(2):
            q = [tile(qp, f, z) for f in range(5)]
            inv = 1.0 / q[0]
            vel = [None] + [q[j] * inv for j in (1, 2, 3)]
            square = vel[1] * vel[1] + vel[2] * vel[2] + vel[3] * vel[3]
            pressure = (GAMMA - 1.0) * (q[4] - 0.5 * q[0] * square)
            out = [gq_s[2 * f + z] for f in range(5)]
            for k, store in ((0, gx_s), (1, gy_s)):
                g = [store[2 * f + z] for f in range(5)]
                u = vel[k + 1]
                dp = (GAMMA - 1.0) * (g[k + 1] + g[4] * u)
                du = (g[1] * q[1] + g[2] * q[2] + g[3] * q[3] + g[4] * (q[4] + pressure)) * inv
                out[0] = out[0] - du * u + 0.5 * dp * square
                for j in (1, 2, 3):
                    out[j] = out[j] + g[j] * u - dp * vel[j]
                out[k + 1] = out[k + 1] + g[0] + du
                out[4] = out[4] + g[4] * u + dp
            for f in range(5):
                after(f, z, out[f] + tile(cqp, f, z))

    grads_one = closure_back(q1p, ctp)

    for s in range(len(stages)):
        speeds = end_stage(spd, s, spd_copies, jnp.maximum)
        if s + 1 < len(stages):
            spd_copies = begin_stage(spd, gsend, grecv, s + 1, speeds)
    for c in a_copies:
        c.wait_recv()

    def keep_middle(f, z, value):
        base = f * 16 + z * 8
        gmp[base : base + 8, :] = 0.25 * tile(ctp, f, z) + 0.25 * TIME_STEP * value

    flux_back(q1p, ctp, 0, 5, 0, 1, speeds[:, 128:256], keep_middle)
    pack(gmp, 15, 3)
    start(c_copies)

    grads_zero = closure_back(q0p, gmp)
    cells = 2 * 8 * 128 * GX * GY * AF
    params = (0.25 * TIME_STEP * grads_one + TIME_STEP * grads_zero) * (1.0 / cells)
    prm_copies = begin_stage(prm, psend, precv, 0, params)

    for c in b_copies + c_copies:
        c.wait_recv()

    def keep_state(f, z, value):
        base = f * 16 + z * 8
        out_ref[base : base + 8, :] = (
            0.75 * tile(ctp, f, z) + tile(gmp, f, z) + TIME_STEP * value
        )

    flux_back(q0p, gmp, 10, 15, 2, 3, speeds[:, 0:128], keep_state)

    for s in range(len(stages)):
        params = end_stage(prm, s, prm_copies, jnp.add)
        if s + 1 < len(stages):
            prm_copies = begin_stage(prm, psend, precv, s + 1, params)
    turned = jnp.transpose(jnp.concatenate([params, jnp.zeros((120, 128), F32)], axis=0))
    gwin_ref[...] = turned[0:64, 0:5]
    gbin_ref[...] = params[5:6, 0:64]
    gbout_ref[...] = params[6:7, 0:5]
    gwout_ref[...] = pltpu.roll(params, 64, 1)[0:5, 0:64]

    for c in started:
        c.wait_send()


def solution(mesh):
    sizes = (mesh.shape["gx"], mesh.shape["gy"], mesh.shape["af"])
    group = sum(sizes) if sizes[0] * sizes[1] * sizes[2] > 16 else sizes[0] * sizes[1] * sizes[2]

    def shards(s0, s1, ct, win, b_in, wout, b_out):
        shape = s0.shape
        vmem = pl.BlockSpec(memory_space=pltpu.VMEM)
        big = pltpu.VMEM((128, 128), F32)
        dma = pltpu.SemaphoreType.DMA
        out, gwin, gbin, gwout, gbout = pl.pallas_call(
            functools.partial(kernel, sizes),
            out_shape=(
                jax.ShapeDtypeStruct((80, 128), F32),
                jax.ShapeDtypeStruct((64, 5), F32),
                jax.ShapeDtypeStruct((1, 64), F32),
                jax.ShapeDtypeStruct((5, 64), F32),
                jax.ShapeDtypeStruct((1, 5), F32),
            ),
            in_specs=[vmem] * 7,
            out_specs=(vmem,) * 5,
            scratch_shapes=[
                big, big, big, big, big, big,
                pltpu.VMEM((64, 32), BF16),
                pltpu.VMEM((64, 32), BF16),
                pltpu.VMEM((16, 256), BF16),
                pltpu.VMEM((8, 128), F32),
                pltpu.VMEM((10, 16, 128), F32),
                pltpu.VMEM((10, 16, 128), F32),
                pltpu.VMEM((10, 8, 256), F32),
                pltpu.VMEM((10, 8, 256), F32),
                pltpu.VMEM((10, 16, 128), F32),
                pltpu.VMEM((10, 8, 256), F32),
                pltpu.VMEM((10, 8, 128), F32),
                pltpu.VMEM((10, 8, 128), F32),
                pltpu.VMEM((10, 8, 128), F32),
                pltpu.VMEM((2, 20, 8, 128), F32),
                pltpu.VMEM((2, 20, 8, 128), F32),
                pltpu.VMEM((4, 8, 128), F32),
                pltpu.VMEM((2, 4, 8, 128), F32),
                pltpu.VMEM((group, 1, 256), F32),
                pltpu.VMEM((group, 8, 128), F32),
                dma((2, 3)), dma((2, 3)), dma((2, 3)), dma((2, 3)),
                dma((group,)), dma((group,)), dma((group,)), dma((group,)),
            ],
            compiler_params=pltpu.CompilerParams(
                collective_id=0, has_side_effects=True, vmem_limit_bytes=32 * 1024 * 1024
            ),
            name="adjoint",
        )(
            s0.reshape(80, 128), s1.reshape(80, 128), ct.reshape(80, 128),
            win, b_in.reshape(1, 64), wout, b_out.reshape(1, 5),
        )
        return out.reshape(shape), gwin, gbin.reshape(64), gwout, gbout.reshape(5)

    field = P(None, "af", ("cases", "gx"), "gy")
    return jax.shard_map(
        shards,
        mesh=mesh,
        in_specs=(field, field, field, P(), P(), P(), P()),
        out_specs=(field, P("cases", None), P("cases"), P("cases", None), P("cases")),
        check_vma=False,
    )
```

time: 169 us -> 29.2 us (0.17)
  blocking collectives: 87.8 us -> 0 us
  other arithmetic: 29.1 us -> 0 us
  starting transfers between devices: 24.9 us -> 0 us
  Pallas kernels: 0 us -> 22.9 us
  matrix products: 8.27 us -> 0 us
  waiting for transfers between devices: 7.65 us -> 0 us
  local copies, waits for them, and re-layouts: 8.23 us -> 5.27 us
  between operations: 2.6 us -> 0.7 us
    psum x1 -> x0, blocking collectives: 57.7 us -> none  [reduce_section(): lax.psum((grads[0], grads[1], grads[2], grads[3]), ('gx', 'gy', 'af'))]
    pmax x1 -> x0, blocking collectives: 30.1 us -> none  [shards(): lax.pmax((max_speed(state_zero), max_speed(state_one)), ('gx', 'gy', 'af'))]
    ppermute x16 -> x0, starting transfers between devices: 24.9 us -> none  [the longest x8 11.7 us: from_behind(): lax.ppermute(array, axis, [(i, (i + by) % count) for i in range(count)])]
    pallas_call x0 -> x1, Pallas kernels: none -> 22.9 us  [shards(): pl.pallas_call(functools.partial(kernel, sizes), out_shape=(jax.ShapeDtyp...]
    add_any x28 -> x0, other arithmetic: 17 us -> none  [the longest x6 5.06 us: weno_face(): cell_c - 2.0 * cell_d + cell_e]
    dot_general x12 -> x0, matrix products: 8.27 us -> none  [the longest x6 5.04 us: closure(): jnp.einsum('fh,h...->f...', weight_out, hidden, precision=lax.Precision.H...]
    mul x20 -> x0, other arithmetic: 7.81 us -> none  [the longest x4 2.22 us: shards(): (0.25 * TIME_STEP * first + TIME_STEP * second) * scale]
    ppermute x16 -> x0, waiting for transfers between devices: 7.65 us -> none  [the longest x4 3.81 us: padded_2(): lax.ppermute(head, axis, [((i + 1) % count, i) for i in range(count)])]
  transfers between devices with their start and end apart: 16 -> 0, of which waited for: 5 -> 0; matrix products, arithmetic and copies ran while one was open for 8% -> 0% of each run, Pallas kernels for 0% -> 0%
where the time goes in v1:
time: 29.2 us; the launch traced here: 28.9 us
  Pallas kernels  22.9 us (78%)
  local copies, waits for them, and re-layouts  5.27 us (18%)
  between operations  0.7 us (2%)
    pallas_call x1, Pallas kernels, shards(): pl.pallas_call(functools.partial(kernel, sizes), out_shape=(jax.ShapeDtyp...  22.9 us
    unnamed x18, local copies, waits for them, and re-layouts  5.27 us

profile of v1, /device:TPU:0, one launch (start us, length us, event | category | flops | bytes accessed | tf_op | source)
XLA Modules:
  0.0 28.9 jit_solution(2186450537463994265)
XLA Ops:
  0.6 0.0 copy-start
  0.6 0.0 copy-start.3
  0.7 0.0 copy-start.4
  0.7 0.0 copy-start.5
  0.7 0.8 %copy.12.win_ref = f32[64,5]{1,0:T(8,128)S(1)} copy(f32[64,5]{0,1:T(8,128)} %param.10) | data formatting | bytes 2560 | tf_op args[3]
  1.5 0.0 copy-done
  1.5 0.0 copy-done.3
  1.5 0.0 copy-done.4
  1.5 0.0 copy-done.5
  1.5 0.0 copy-start.1
  1.5 0.8 %copy-done.1 = f32[5,2,8,128]{3,2,1,0:T(8,128)S(1)} copy-done((f32[5,2,8,128]{3,2,1,0:T(8,128)S(1)}, f32[5,2,8,128]{3,2,1,0:T(8,128)}, u32[]{:S(2)}) %copy-start.1) | copy-done | bytes 40984
  2.3 0.0 copy-start.2
  2.3 0.8 %copy-done.2 = f32[5,2,8,128]{3,2,1,0:T(8,128)S(1)} copy-done((f32[5,2,8,128]{3,2,1,0:T(8,128)S(1)}, f32[5,2,8,128]{3,2,1,0:T(8,128)}, u32[]{:S(2)}) %copy-start.2) | copy-done | bytes 40984
  3.1 22.9 %adjoint.1 = (f32[80,128]{1,0:T(8,128)S(1)}, f32[64,5]{1,0:T(8,128)S(1)}, f32[1,64]{1,0:T(1,128)S(1)}, f32[5,64]{1,0:T(8,128)S(1)}, f32[1,5]{1,0:T(1,128)S(1)}) custom-call(f32[80,128]{1,0:T(8,128)S(1)} %bitcast.8, f32[80,128]{1,0:T(8,128)S(1)} %bitcast.9, f32[80,128]{1,0:T(8,128)S(1)} %bitcast.10, f32[64,5]{1,0:T(8,128)S(1)} %copy.12.win_ref, ...), custom_call_target="tpu_custom_call" | custom-call | tf_op jit(solution)/shard_map/adjoint/pallas_call | solution.py:473
  26.0 0.7 %copy.13 = f32[64,5]{0,1:T(8,128)} copy(f32[64,5]{1,0:T(8,128)S(1)} %get-tuple-element.16) | data formatting | bytes 2560
  26.7 0.6 %copy.18 = f32[5,2,8,128]{3,2,1,0:T(8,128)} copy(f32[5,2,8,128]{3,2,1,0:T(8,128)S(1)} %bitcast.11) | data formatting | bytes 81920
  27.3 0.5 %copy.19 = f32[64]{0:T(128)} copy(f32[64]{0:T(128)S(1)} %bitcast.15) | data formatting | bytes 512
  27.8 0.6 %copy.20 = f32[5,64]{1,0:T(8,128)} copy(f32[5,64]{1,0:T(8,128)S(1)} %get-tuple-element.28) | data formatting | bytes 2560
  28.4 0.5 %copy.21 = f32[5]{0:T(128)} copy(f32[5]{0:T(128)S(1)} %bitcast.14) | data formatting | bytes 40
Async XLA Ops:
  0.6 0.8 %copy-start = (f32[5,2,8,128]{3,2,1,0:T(8,128)S(1)}, f32[5,2,8,128]{3,2,1,0:T(8,128)}, u32[]{:S(2)}) copy-start(f32[5,2,8,128]{3,2,1,0:T(8,128)} %param.7) | copy-start | bytes 122884
  0.6 0.8 %copy-start.3 = (f32[5,64]{1,0:T(8,128)S(1)}, f32[5,64]{1,0:T(8,128)}, u32[]{:S(2)}) copy-start(f32[5,64]{1,0:T(8,128)} %wout_ref.1) | copy-start | bytes 3844
  0.7 0.8 %copy-start.4 = (f32[64]{0:T(128)S(1)}, f32[64]{0:T(128)}, u32[]{:S(2)}) copy-start(f32[64]{0:T(128)} %param.11) | copy-start | bytes 772
  0.7 0.8 %copy-start.5 = (f32[5]{0:T(128)S(1)}, f32[5]{0:T(128)}, u32[]{:S(2)}) copy-start(f32[5]{0:T(128)} %param.13) | copy-start | bytes 64
  1.5 0.8 %copy-start.1 = (f32[5,2,8,128]{3,2,1,0:T(8,128)S(1)}, f32[5,2,8,128]{3,2,1,0:T(8,128)}, u32[]{:S(2)}) copy-start(f32[5,2,8,128]{3,2,1,0:T(8,128)} %param.8) | copy-start | bytes 122884
  2.3 0.8 %copy-start.2 = (f32[5,2,8,128]{3,2,1,0:T(8,128)S(1)}, f32[5,2,8,128]{3,2,1,0:T(8,128)}, u32[]{:S(2)}) copy-start(f32[5,2,8,128]{3,2,1,0:T(8,128)} %param.9) | copy-start | bytes 122884

commit v2 on v1

--- a/solution.py
+++ b/solution.py
@@ -25,7 +25,11 @@
     return high, x - high
 
 
-def weno_grads(d0, d1, d2, d3, w):
+def inverse(x):
+    return pl.reciprocal(x, approx=True)
+
+
+def weno_grads(d0, d1, d2, d3):
     a0 = 8.0 * d0 - 11.0 * d1
     a1 = 20.0 * d1 - 11.0 * d0
     b0 = 8.0 * d1 - 5.0 * d2
@@ -33,21 +37,20 @@
     c0 = 20.0 * d2 - 11.0 * d3
     c1 = 8.0 * d3 - 11.0 * d2
     eps = 6.0 * WENO_EPS
-    ra = 1.0 / (eps + d0 * a0 + d1 * a1)
-    rb = 1.0 / (eps + d1 * b0 + d2 * b1)
-    rc = 1.0 / (eps + d2 * c0 + d3 * c1)
+    ra = inverse(eps + (d0 * a0 + d1 * a1))
+    rb = inverse(eps + (d1 * b0 + d2 * b1))
+    rc = inverse(eps + (d2 * c0 + d3 * c1))
     wa = ra * ra
     wb = 6.0 * (rb * rb)
     wc = 3.0 * (rc * rc)
     ga = 5.0 * d1 - 2.0 * d0
     gb = d1 + 2.0 * d2
     gc = 4.0 * d2 - d3
-    inv = 1.0 / (wa + wb + wc)
+    inv = inverse(wa + wb + wc)
     mean = (wa * ga + wb * gb + wc * gc) * inv
-    scale = w * inv
-    ka = wa * scale
-    kb = wb * scale
-    kc = wc * scale
+    ka = wa * inv
+    kb = wb * inv
+    kc = wc * inv
     ma = 4.0 * ka * ra * (mean - ga)
     mb = 4.0 * kb * rb * (mean - gb)
     mc = 4.0 * kc * rc * (mean - gc)
@@ -59,27 +62,32 @@
     )
 
 
-def line_adjoint(up, down, v, axis, own):
+def line_grads(up, down, axis):
     sh = functools.partial(shifted, axis=axis)
-    w = sh(v, 1) - v
+    d = sh(up, 1) - up
+    e = down - sh(down, 1)
+    return weno_grads(sh(d, -2), sh(d, -1), d, sh(d, 1)), weno_grads(sh(e, 2), sh(e, 1), e, sh(e, -1))
+
+
+def line_adjoint(grads, v, axis, own):
+    sh = functools.partial(shifted, axis=axis)
+    ahead = sh(v, 1)
+    w = ahead - v
     w6 = w * (1.0 / 6.0)
-    d = sh(up, 1) - up
-    g = weno_grads(sh(d, -2), sh(d, -1), d, sh(d, 1), w6)
-    gp = sh(g[0], 2) + sh(g[1], 1) + g[2] + sh(g[3], -1)
-    d = down - sh(down, 1)
-    g = weno_grads(sh(d, 2), sh(d, 1), d, sh(d, -1), w6)
-    gm = sh(g[0], -2) + sh(g[1], -1) + g[2] + sh(g[3], 1)
     wb = sh(w, -1)
+    g = [w6 * x for x in grads[0]]
+    gp = sh(sh(g[0], 1) + g[1], 1) + g[2] + sh(g[3], -1)
+    g = [w6 * x for x in grads[1]]
+    gm = sh(sh(g[0], -1) + g[1], -1) + g[2] + sh(g[3], 1)
     t = gp - gm
     s = gp + gm
     total = w + wb + sh(t, -1) - t
     apart = w - wb + sh(s, -1) - s
-    laplace = sh(v, 1) + sh(v, -1) - 2.0 * v
-    return own(total), own(apart), own(laplace)
+    return own(total), own(apart), own(w - wb)
 
 
 def flux_parts(q, k):
-    inv = 1.0 / q[0]
+    inv = inverse(q[0])
     pressure = (GAMMA - 1.0) * (
         q[4] - 0.5 * (q[1] * q[1] + q[2] * q[2] + q[3] * q[3]) * inv
     )
@@ -94,7 +102,7 @@
     s0_ref, s1_ref, ct_ref, win_ref, bin_ref, wout_ref, bout_ref,
     out_ref, gwin_ref, gbin_ref, gwout_ref, gbout_ref,
     q0p, q1p, ctp, gmp, cqp, wtile, w1, w2, w3, bcol,
-    fxp, fxm, fyp, fym, vx, vy, gx_s, gy_s, gq_s,
+    fxp, fxm, fyp, fym, kx, ky, vx, vy, gx_s, gy_s, gq_s,
     xs, xr, ys, yr, spd, prm,
     xsend, xrecv, ysend, yrecv, gsend, grecv, psend, precv,
 ):
@@ -209,7 +217,7 @@
         best = None
         for z in range(2):
             q = [tile(ref, f, z) for f in range(5)]
-            inv = 1.0 / q[0]
+            inv = inverse(q[0])
             pressure = (GAMMA - 1.0) * (
                 q[4] - 0.5 * (q[1] * q[1] + q[2] * q[2] + q[3] * q[3]) * inv
             )
@@ -356,13 +364,12 @@
         d = jnp.sum(jnp.where(lane == row, d, 0.0), axis=0, keepdims=True)
         return jnp.where(row == 6, d, total)
 
-    def flux_back(qp, cp, xq, xc, yq, yc, speed, after):
+    def flux_parts_of(qp, xq, yq, speed):
         speed8 = jnp.broadcast_to(speed, (8, 128))
         speed16 = jnp.broadcast_to(speed, (16, 128))
         speed256 = jnp.concatenate([speed8, speed8], axis=1)
         hx = [x_halo(xq, f) for f in range(5)]
-        cx = [x_halo(xc, f) for f in range(5)]
-        pq, pc = y_packed(yq), y_packed(yc)
+        pq = y_packed(yq)
         for z in range(2):
             own = [tile(qp, f, z) for f in range(5)]
             q = [jnp.concatenate([own[f], hx[f][z]], axis=0) for f in range(5)]
@@ -375,18 +382,44 @@
                 lead = speed256 * q[f]
                 fyp[2 * f + z] = 0.5 * (part + lead)
                 fym[2 * f + z] = 0.5 * (part - lead)
-            for f in range(5):
+
+    def fill_v(cp, xc, yc):
+        pc = y_packed(yc)
+        for f in range(5):
+            hx = x_halo(xc, f)
+            for z in range(2):
                 t = 2 * f + z
                 v = tile(cp, f, z)
                 vx[t, 0:8, :] = v
-                vx[t, 8:16, :] = cx[f][z]
+                vx[t, 8:16, :] = hx[z]
                 vy[t, :, 0:128] = v
                 vy[t, :, 128:256] = y_halo(pc, f, z)
 
+    def grads_of(t):
+        return line_grads(fxp[t], fxm[t], 0), line_grads(fyp[t], fym[t], 1)
+
+    def keep_grads(t, _):
+        along_x, along_y = grads_of(t)
+        for side in range(2):
+            for k in range(4):
+                kx[t, side, k] = along_x[side][k]
+                ky[t, side, k] = along_y[side][k]
+        return 0
+
+    def kept_grads(t):
+        return (
+            [[kx[t, side, k] for k in range(4)] for side in range(2)],
+            [[ky[t, side, k] for k in range(4)] for side in range(2)],
+        )
+
+    def flux_back(qp, grads_at, speed, after):
+        speed8 = jnp.broadcast_to(speed, (8, 128))
+
         def body(t, _):
-            total, apart, laplace = line_adjoint(fxp[t], fxm[t], vx[t], 0, lambda x: x[0:8, :])
+            along_x, along_y = grads_at(t)
+            total, apart, laplace = line_adjoint(along_x, vx[t], 0, lambda x: x[0:8, :])
             gx_s[t] = 0.5 * total
-            total_y, apart_y, laplace_y = line_adjoint(fyp[t], fym[t], vy[t], 1, lambda x: x[:, 0:128])
+            total_y, apart_y, laplace_y = line_adjoint(along_y, vy[t], 1, lambda x: x[:, 0:128])
             gy_s[t] = 0.5 * total_y
             viscous = jnp.where(t < 2, 0.0, VISCOSITY).astype(F32)
             gq_s[t] = 0.5 * speed8 * (apart + apart_y) + viscous * (laplace + laplace_y)
@@ -396,7 +429,7 @@
 
         for z in range(2):
             q = [tile(qp, f, z) for f in range(5)]
-            inv = 1.0 / q[0]
+            inv = inverse(q[0])
             vel = [None] + [q[j] * inv for j in (1, 2, 3)]
             square = vel[1] * vel[1] + vel[2] * vel[2] + vel[3] * vel[3]
             pressure = (GAMMA - 1.0) * (q[4] - 0.5 * q[0] * square)
@@ -427,7 +460,9 @@
         base = f * 16 + z * 8
         gmp[base : base + 8, :] = 0.25 * tile(ctp, f, z) + 0.25 * TIME_STEP * value
 
-    flux_back(q1p, ctp, 0, 5, 0, 1, speeds[:, 128:256], keep_middle)
+    flux_parts_of(q1p, 0, 0, speeds[:, 128:256])
+    fill_v(ctp, 5, 1)
+    flux_back(q1p, grads_of, speeds[:, 128:256], keep_middle)
     pack(gmp, 15, 3)
     start(c_copies)
 
@@ -436,8 +471,13 @@
     params = (0.25 * TIME_STEP * grads_one + TIME_STEP * grads_zero) * (1.0 / cells)
     prm_copies = begin_stage(prm, psend, precv, 0, params)
 
-    for c in b_copies + c_copies:
+    for c in b_copies:
         c.wait_recv()
+    flux_parts_of(q0p, 10, 2, speeds[:, 0:128])
+    lax.fori_loop(0, 10, keep_grads, 0)
+    for c in c_copies:
+        c.wait_recv()
+    fill_v(gmp, 15, 3)
 
     def keep_state(f, z, value):
         base = f * 16 + z * 8
@@ -445,7 +485,7 @@
             0.75 * tile(ctp, f, z) + tile(gmp, f, z) + TIME_STEP * value
         )
 
-    flux_back(q0p, gmp, 10, 15, 2, 3, speeds[:, 0:128], keep_state)
+    flux_back(q0p, kept_grads, speeds[:, 0:128], keep_state)
 
     for s in range(len(stages)):
         params = end_stage(prm, s, prm_copies, jnp.add)
@@ -491,6 +531,8 @@
                 pltpu.VMEM((10, 16, 128), F32),
                 pltpu.VMEM((10, 8, 256), F32),
                 pltpu.VMEM((10, 8, 256), F32),
+                pltpu.VMEM((10, 2, 4, 16, 128), F32),
+                pltpu.VMEM((10, 2, 4, 8, 256), F32),
                 pltpu.VMEM((10, 16, 128), F32),
                 pltpu.VMEM((10, 8, 256), F32),
                 pltpu.VMEM((10, 8, 128), F32),

time: 29.2 us -> 29.4 us (level)
  no operation moved by 1% of the time
where the time goes in v2:
time: 29.4 us; the launch traced here: 29.1 us
  Pallas kernels  23.1 us (79%)
  local copies, waits for them, and re-layouts  5.27 us (18%)
  between operations  0.7 us (2%)
    pallas_call x1, Pallas kernels, shards(): pl.pallas_call(functools.partial(kernel, sizes), out_shape=(jax.ShapeDtyp...  23.1 us
    unnamed x18, local copies, waits for them, and re-layouts  5.27 us

profile of v2, /device:TPU:0, one launch (start us, length us, event | category | flops | bytes accessed | tf_op | source)
XLA Modules:
  0.0 29.1 jit_solution(15971360150681134822)
XLA Ops:
  0.6 0.0 copy-start
  0.6 0.0 copy-start.3
  0.7 0.0 copy-start.4
  0.7 0.0 copy-start.5
  0.7 0.8 %copy.12.win_ref = f32[64,5]{1,0:T(8,128)S(1)} copy(f32[64,5]{0,1:T(8,128)} %param.10) | data formatting | bytes 2560 | tf_op args[3]
  1.5 0.0 copy-done
  1.5 0.0 copy-done.3
  1.5 0.0 copy-done.4
  1.5 0.0 copy-done.5
  1.5 0.0 copy-start.1
  1.5 0.8 %copy-done.1 = f32[5,2,8,128]{3,2,1,0:T(8,128)S(1)} copy-done((f32[5,2,8,128]{3,2,1,0:T(8,128)S(1)}, f32[5,2,8,128]{3,2,1,0:T(8,128)}, u32[]{:S(2)}) %copy-start.1) | copy-done | bytes 40984
  2.3 0.0 copy-start.2
  2.3 0.8 %copy-done.2 = f32[5,2,8,128]{3,2,1,0:T(8,128)S(1)} copy-done((f32[5,2,8,128]{3,2,1,0:T(8,128)S(1)}, f32[5,2,8,128]{3,2,1,0:T(8,128)}, u32[]{:S(2)}) %copy-start.2) | copy-done | bytes 40984
  3.1 23.1 %adjoint.1 = (f32[80,128]{1,0:T(8,128)S(1)}, f32[64,5]{1,0:T(8,128)S(1)}, f32[1,64]{1,0:T(1,128)S(1)}, f32[5,64]{1,0:T(8,128)S(1)}, f32[1,5]{1,0:T(1,128)S(1)}) custom-call(f32[80,128]{1,0:T(8,128)S(1)} %bitcast.8, f32[80,128]{1,0:T(8,128)S(1)} %bitcast.9, f32[80,128]{1,0:T(8,128)S(1)} %bitcast.10, f32[64,5]{1,0:T(8,128)S(1)} %copy.12.win_ref, ...), custom_call_target="tpu_custom_call" | custom-call | tf_op jit(solution)/shard_map/adjoint/pallas_call | solution.py:513
  26.2 0.7 %copy.13 = f32[64,5]{0,1:T(8,128)} copy(f32[64,5]{1,0:T(8,128)S(1)} %get-tuple-element.16) | data formatting | bytes 2560
  26.9 0.6 %copy.18 = f32[5,2,8,128]{3,2,1,0:T(8,128)} copy(f32[5,2,8,128]{3,2,1,0:T(8,128)S(1)} %bitcast.11) | data formatting | bytes 81920
  27.5 0.5 %copy.19 = f32[64]{0:T(128)} copy(f32[64]{0:T(128)S(1)} %bitcast.15) | data formatting | bytes 512
  28.0 0.6 %copy.20 = f32[5,64]{1,0:T(8,128)} copy(f32[5,64]{1,0:T(8,128)S(1)} %get-tuple-element.28) | data formatting | bytes 2560
  28.6 0.5 %copy.21 = f32[5]{0:T(128)} copy(f32[5]{0:T(128)S(1)} %bitcast.14) | data formatting | bytes 40
Async XLA Ops:
  0.6 0.8 %copy-start = (f32[5,2,8,128]{3,2,1,0:T(8,128)S(1)}, f32[5,2,8,128]{3,2,1,0:T(8,128)}, u32[]{:S(2)}) copy-start(f32[5,2,8,128]{3,2,1,0:T(8,128)} %param.7) | copy-start | bytes 122884
  0.6 0.8 %copy-start.3 = (f32[5,64]{1,0:T(8,128)S(1)}, f32[5,64]{1,0:T(8,128)}, u32[]{:S(2)}) copy-start(f32[5,64]{1,0:T(8,128)} %wout_ref.1) | copy-start | bytes 3844
  0.7 0.8 %copy-start.4 = (f32[64]{0:T(128)S(1)}, f32[64]{0:T(128)}, u32[]{:S(2)}) copy-start(f32[64]{0:T(128)} %param.11) | copy-start | bytes 772
  0.7 0.8 %copy-start.5 = (f32[5]{0:T(128)S(1)}, f32[5]{0:T(128)}, u32[]{:S(2)}) copy-start(f32[5]{0:T(128)} %param.13) | copy-start | bytes 64
  1.5 0.8 %copy-start.1 = (f32[5,2,8,128]{3,2,1,0:T(8,128)S(1)}, f32[5,2,8,128]{3,2,1,0:T(8,128)}, u32[]{:S(2)}) copy-start(f32[5,2,8,128]{3,2,1,0:T(8,128)} %param.8) | copy-start | bytes 122884
  2.3 0.8 %copy-start.2 = (f32[5,2,8,128]{3,2,1,0:T(8,128)S(1)}, f32[5,2,8,128]{3,2,1,0:T(8,128)}, u32[]{:S(2)}) copy-start(f32[5,2,8,128]{3,2,1,0:T(8,128)} %param.9) | copy-start | bytes 122884

commit v3 on v2

--- a/solution.py
+++ b/solution.py
@@ -99,8 +99,9 @@
 
 def kernel(
     sizes,
-    s0_ref, s1_ref, ct_ref, win_ref, bin_ref, wout_ref, bout_ref,
-    out_ref, gwin_ref, gbin_ref, gwout_ref, gbout_ref,
+    s0_hbm, s1_hbm, ct_hbm, win_hbm, bin_hbm, wout_hbm, bout_hbm,
+    out_ref,
+    win_ref, bin_ref, wout_ref, bout_ref, in_sem,
     q0p, q1p, ctp, gmp, cqp, wtile, w1, w2, w3, bcol,
     fxp, fxm, fyp, fym, kx, ky, vx, vy, gx_s, gy_s, gq_s,
     xs, xr, ys, yr, spd, prm,
@@ -127,6 +128,14 @@
             lax.rem(ia + off[2], AF) if off[2] else ia,
         )
 
+    loads = []
+    for n, (src, dst) in enumerate((
+        (s1_hbm, q1p.at[0:80]), (ct_hbm, ctp.at[0:80]), (s0_hbm, q0p.at[0:80]),
+        (win_hbm, win_ref), (bin_hbm, bin_ref), (wout_hbm, wout_ref), (bout_hbm, bout_ref),
+    )):
+        loads.append(pltpu.make_async_copy(src, dst, in_sem.at[n]))
+        loads[-1].start()
+
     barrier = pltpu.get_barrier_semaphore()
     greeted = 0
     for stage in stages:
@@ -139,8 +148,6 @@
     upper = row < 4
 
     ones = jnp.ones((16, 128), F32)
-    for ref, src in ((q0p, s0_ref), (q1p, s1_ref), (ctp, ct_ref)):
-        ref[0:80, :] = src[...]
     for ref in (q0p, q1p):
         ref[80:96, :] = ones
         ref[96:128, :] = jnp.zeros((32, 128), F32)
@@ -209,8 +216,11 @@
     def y_halo(packed, f, z):
         return pltpu.roll(packed, (-(4 + 8 * (f * 2 + z))) % 128, 1)
 
+    loads[0].wait()
     pack(q1p, 0, 0)
+    loads[1].wait()
     pack(ctp, 5, 1)
+    loads[2].wait()
     pack(q0p, 10, 2)
 
     def top_speed(ref):
@@ -229,10 +239,11 @@
 
     fastest = jnp.concatenate([top_speed(q0p), top_speed(q1p)], axis=1)
 
-    wtile[...] = jnp.zeros_like(wtile)
-    wtile[0:64, 0:5] = win_ref[...]
-    wint = jnp.transpose(wtile[...])[0:8, :]
     wtile[0:8, :] = jnp.zeros((8, 128), F32)
+    for c in loads[3:]:
+        c.wait()
+    wtile[0:5, 0:64] = win_ref[...]
+    wint = wtile[0:8, :]
     wtile[0:5, 0:64] = wout_ref[...]
     wout8 = wtile[0:8, :]
     wtile[0:8, :] = jnp.zeros((8, 128), F32)
@@ -425,7 +436,7 @@
             gq_s[t] = 0.5 * speed8 * (apart + apart_y) + viscous * (laplace + laplace_y)
             return 0
 
-        lax.fori_loop(0, 10, body, 0)
+        lax.fori_loop(0, 10, body, 0, unroll=5)
 
         for z in range(2):
             q = [tile(qp, f, z) for f in range(5)]
@@ -491,14 +502,21 @@
         params = end_stage(prm, s, prm_copies, jnp.add)
         if s + 1 < len(stages):
             prm_copies = begin_stage(prm, psend, precv, s + 1, params)
-    turned = jnp.transpose(jnp.concatenate([params, jnp.zeros((120, 128), F32)], axis=0))
-    gwin_ref[...] = turned[0:64, 0:5]
+    out_ref[80:88, :] = params
+
+    for c in started:
+        c.wait_send()
+
+
+def spread(packed_ref, out_ref, gwin_ref, gbin_ref, gwout_ref, gbout_ref, sem):
+    whole = pltpu.make_async_copy(packed_ref.at[0:80], out_ref, sem)
+    whole.start()
+    params = packed_ref[80:88, :]
+    gwin_ref[...] = params[0:5, 0:64]
     gbin_ref[...] = params[5:6, 0:64]
     gbout_ref[...] = params[6:7, 0:5]
     gwout_ref[...] = pltpu.roll(params, 64, 1)[0:5, 0:64]
-
-    for c in started:
-        c.wait_send()
+    whole.wait()
 
 
 def solution(mesh):
@@ -510,18 +528,15 @@
         vmem = pl.BlockSpec(memory_space=pltpu.VMEM)
         big = pltpu.VMEM((128, 128), F32)
         dma = pltpu.SemaphoreType.DMA
-        out, gwin, gbin, gwout, gbout = pl.pallas_call(
+        hbm = pl.BlockSpec(memory_space=pltpu.MemorySpace.HBM)
+        packed = pl.pallas_call(
             functools.partial(kernel, sizes),
-            out_shape=(
-                jax.ShapeDtypeStruct((80, 128), F32),
-                jax.ShapeDtypeStruct((64, 5), F32),
-                jax.ShapeDtypeStruct((1, 64), F32),
-                jax.ShapeDtypeStruct((5, 64), F32),
-                jax.ShapeDtypeStruct((1, 5), F32),
-            ),
-            in_specs=[vmem] * 7,
-            out_specs=(vmem,) * 5,
+            out_shape=jax.ShapeDtypeStruct((88, 128), F32),
+            in_specs=[hbm] * 7,
+            out_specs=vmem,
             scratch_shapes=[
+                pltpu.VMEM((5, 64), F32), pltpu.VMEM((1, 64), F32),
+                pltpu.VMEM((5, 64), F32), pltpu.VMEM((1, 5), F32), dma((7,)),
                 big, big, big, big, big, big,
                 pltpu.VMEM((64, 32), BF16),
                 pltpu.VMEM((64, 32), BF16),
@@ -548,14 +563,28 @@
                 dma((group,)), dma((group,)), dma((group,)), dma((group,)),
             ],
             compiler_params=pltpu.CompilerParams(
-                collective_id=0, has_side_effects=True, vmem_limit_bytes=32 * 1024 * 1024
+                collective_id=0, has_side_effects=True, vmem_limit_bytes=64 * 1024 * 1024
             ),
             name="adjoint",
         )(
             s0.reshape(80, 128), s1.reshape(80, 128), ct.reshape(80, 128),
-            win, b_in.reshape(1, 64), wout, b_out.reshape(1, 5),
+            win.T, b_in.reshape(1, 64), wout, b_out.reshape(1, 5),
         )
-        return out.reshape(shape), gwin, gbin.reshape(64), gwout, gbout.reshape(5)
+        out, gwin, gbin, gwout, gbout = pl.pallas_call(
+            spread,
+            out_shape=(
+                jax.ShapeDtypeStruct((80, 128), F32),
+                jax.ShapeDtypeStruct((5, 64), F32),
+                jax.ShapeDtypeStruct((1, 64), F32),
+                jax.ShapeDtypeStruct((5, 64), F32),
+                jax.ShapeDtypeStruct((1, 5), F32),
+            ),
+            in_specs=[vmem],
+            out_specs=(hbm, vmem, vmem, vmem, vmem),
+            scratch_shapes=[dma(())],
+            name="spread",
+        )(packed)
+        return out.reshape(shape), gwin.T, gbin.reshape(64), gwout, gbout.reshape(5)
 
     field = P(None, "af", ("cases", "gx"), "gy")
     return jax.shard_map(

time: 29.4 us -> 22 us (0.75)
  local copies, waits for them, and re-layouts: 5.27 us -> 0 us
  Pallas kernels: 23.1 us -> 21.1 us
    unnamed x18 -> x0, local copies, waits for them, and re-layouts: 5.27 us -> none
    pallas_call x1 -> x2, Pallas kernels: 23.1 us -> 21.1 us  [the longest x1 19.1 us: shards(): pl.pallas_call(functools.partial(kernel, sizes), out_shape=jax.ShapeDtype...]
where the time goes in v3:
time: 22 us; the launch traced here: 21.8 us
  Pallas kernels  21.1 us (96%)
  between operations  0.64 us (3%)
    pallas_call x1, Pallas kernels, shards(): pl.pallas_call(functools.partial(kernel, sizes), out_shape=jax.ShapeDtype...  19.1 us
    pallas_call x1, Pallas kernels, shards(): pl.pallas_call(spread, out_shape=(jax.ShapeDtypeStruct((80, 128), F32), j...  2.02 us

profile of v3, /device:TPU:0, one launch (start us, length us, event | category | flops | bytes accessed | tf_op | source)
XLA Modules:
  0.0 21.8 jit_solution(10765389314940811539)
XLA Ops:
  0.6 19.1 %adjoint.1.packed_ref = f32[88,128]{1,0:T(8,128)} custom-call(f32[80,128]{1,0:T(8,128)} %bitcast.10, f32[80,128]{1,0:T(8,128)} %bitcast.11, f32[80,128]{1,0:T(8,128)} %bitcast.12, f32[5,64]{1,0:T(8,128)} %bitcast.13, f32[1,64]{1,0:T(1,128)} %bitcast.14, f32[5,64]{1,0:T(8,128)} %wout_hbm.1, f32[1,5]{1,0:T(1,128)} %bitcast.15), custom_call_target="tpu_custom_call" | custom-call | tf_op jit(solution)/shard_map/adjoint/pallas_call | solution.py:532
  19.8 2.0 %spread.1 = (f32[80,128]{1,0:T(8,128)}, f32[5,64]{1,0:T(8,128)}, f32[1,64]{1,0:T(1,128)}, f32[5,64]{1,0:T(8,128)}, f32[1,5]{1,0:T(1,128)}) custom-call(f32[88,128]{1,0:T(8,128)} %adjoint.1.packed_ref), custom_call_target="tpu_custom_call" | custom-call | tf_op jit(solution)/shard_map/spread/pallas_call | solution.py:573

commit v4 on v3

--- a/solution.py
+++ b/solution.py
@@ -130,7 +130,7 @@
 
     loads = []
     for n, (src, dst) in enumerate((
-        (s1_hbm, q1p.at[0:80]), (ct_hbm, ctp.at[0:80]), (s0_hbm, q0p.at[0:80]),
+        (s1_hbm, q1p.at[0:80]), (s0_hbm, q0p.at[0:80]), (ct_hbm, ctp.at[0:80]),
         (win_hbm, win_ref), (bin_hbm, bin_ref), (wout_hbm, wout_ref), (bout_hbm, bout_ref),
     )):
         loads.append(pltpu.make_async_copy(src, dst, in_sem.at[n]))
@@ -216,12 +216,6 @@
     def y_halo(packed, f, z):
         return pltpu.roll(packed, (-(4 + 8 * (f * 2 + z))) % 128, 1)
 
-    loads[0].wait()
-    pack(q1p, 0, 0)
-    loads[1].wait()
-    pack(ctp, 5, 1)
-    loads[2].wait()
-    pack(q0p, 10, 2)
 
     def top_speed(ref):
         best = None
@@ -237,7 +231,72 @@
         best = jnp.max(best, axis=0, keepdims=True)
         return jnp.broadcast_to(jnp.max(best, axis=1, keepdims=True), (1, 128))
 
+    loads[0].wait()
+    loads[1].wait()
     fastest = jnp.concatenate([top_speed(q0p), top_speed(q1p)], axis=1)
+
+    loads[2].wait()
+    pack(q1p, 0, 0)
+    pack(ctp, 5, 1)
+    pl.semaphore_wait(barrier, greeted)
+
+    a_copies = x_copies(0, 10, 0) + y_copies(0, 2, 0)
+    b_copies = x_copies(10, 5, 1) + y_copies(2, 1, 1)
+    c_copies = x_copies(15, 5, 2) + y_copies(3, 1, 2)
+
+    def numbers(stage_index):
+        base = sum(len(stages[s]) for s in range(stage_index))
+        return [base + k for k in range(len(stages[stage_index]))]
+
+    def my_rank(stage_index):
+        if joint:
+            return (ix * GY + iy) * AF + ia
+        return (ix, iy, ia)[stage_index]
+
+    def group_copies(buf, send, recv, stage_index):
+        base = numbers(stage_index)[0]
+        rank = base + my_rank(stage_index)
+        made = []
+        for k, off in enumerate(stages[stage_index]):
+            if k == 0:
+                continue
+            made.append(
+                pltpu.make_async_remote_copy(
+                    src_ref=buf.at[rank],
+                    dst_ref=buf.at[rank],
+                    send_sem=send.at[base + k],
+                    recv_sem=recv.at[base + k],
+                    device_id=place(off),
+                    device_id_type=MESH,
+                )
+            )
+        return made
+
+    started = []
+
+    def start(copies):
+        for c in copies:
+            c.start()
+            started.append(c)
+
+    def begin_stage(buf, send, recv, s, value):
+        buf[numbers(s)[0] + my_rank(s)] = value
+        copies = group_copies(buf, send, recv, s)
+        start(copies)
+        return copies
+
+    def end_stage(buf, s, copies, op):
+        for c in copies:
+            c.wait_recv()
+        total = None
+        for n in numbers(s):
+            total = buf[n] if total is None else op(total, buf[n])
+        return total
+
+    spd_copies = begin_stage(spd, gsend, grecv, 0, fastest)
+    start(a_copies)
+    pack(q0p, 10, 2)
+    start(b_copies)
 
     wtile[0:8, :] = jnp.zeros((8, 128), F32)
     for c in loads[3:]:
@@ -268,64 +327,6 @@
         (8, 128),
     )
 
-    pl.semaphore_wait(barrier, greeted)
-
-    a_copies = x_copies(0, 10, 0) + y_copies(0, 2, 0)
-    b_copies = x_copies(10, 5, 1) + y_copies(2, 1, 1)
-    c_copies = x_copies(15, 5, 2) + y_copies(3, 1, 2)
-
-    def numbers(stage_index):
-        base = sum(len(stages[s]) for s in range(stage_index))
-        return [base + k for k in range(len(stages[stage_index]))]
-
-    def my_rank(stage_index):
-        if joint:
-            return (ix * GY + iy) * AF + ia
-        return (ix, iy, ia)[stage_index]
-
-    def group_copies(buf, send, recv, stage_index):
-        base = numbers(stage_index)[0]
-        rank = base + my_rank(stage_index)
-        made = []
-        for k, off in enumerate(stages[stage_index]):
-            if k == 0:
-                continue
-            made.append(
-                pltpu.make_async_remote_copy(
-                    src_ref=buf.at[rank],
-                    dst_ref=buf.at[rank],
-                    send_sem=send.at[base + k],
-                    recv_sem=recv.at[base + k],
-                    device_id=place(off),
-                    device_id_type=MESH,
-                )
-            )
-        return made
-
-    started = []
-
-    def start(copies):
-        for c in copies:
-            c.start()
-            started.append(c)
-
-    def begin_stage(buf, send, recv, s, value):
-        buf[numbers(s)[0] + my_rank(s)] = value
-        copies = group_copies(buf, send, recv, s)
-        start(copies)
-        return copies
-
-    def end_stage(buf, s, copies, op):
-        for c in copies:
-            c.wait_recv()
-        total = None
-        for n in numbers(s):
-            total = buf[n] if total is None else op(total, buf[n])
-        return total
-
-    spd_copies = begin_stage(spd, gsend, grecv, 0, fastest)
-    start(a_copies)
-    start(b_copies)
 
     def closure_back(qp, cp):
         acc = jnp.zeros((32, 256), F32)

time: 22 us -> 22 us (level)
  no operation moved by 1% of the time
where the time goes in v4:
time: 22 us; the launch traced here: 21.8 us
  Pallas kernels  21.1 us (96%)
  between operations  0.64 us (3%)
    pallas_call x1, Pallas kernels, shards(): pl.pallas_call(functools.partial(kernel, sizes), out_shape=jax.ShapeDtype...  19.1 us
    pallas_call x1, Pallas kernels, shards(): pl.pallas_call(spread, out_shape=(jax.ShapeDtypeStruct((80, 128), F32), j...  2.02 us

profile of v4, /device:TPU:0, one launch (start us, length us, event | category | flops | bytes accessed | tf_op | source)
XLA Modules:
  0.0 21.8 jit_solution(7318112436750283366)
XLA Ops:
  0.6 19.1 %adjoint.1.packed_ref = f32[88,128]{1,0:T(8,128)} custom-call(f32[80,128]{1,0:T(8,128)} %bitcast.10, f32[80,128]{1,0:T(8,128)} %bitcast.11, f32[80,128]{1,0:T(8,128)} %bitcast.12, f32[5,64]{1,0:T(8,128)} %bitcast.13, f32[1,64]{1,0:T(1,128)} %bitcast.14, f32[5,64]{1,0:T(8,128)} %wout_hbm.1, f32[1,5]{1,0:T(1,128)} %bitcast.15), custom_call_target="tpu_custom_call" | custom-call | tf_op jit(solution)/shard_map/adjoint/pallas_call | solution.py:533
  19.8 2.0 %spread.1 = (f32[80,128]{1,0:T(8,128)}, f32[5,64]{1,0:T(8,128)}, f32[1,64]{1,0:T(1,128)}, f32[5,64]{1,0:T(8,128)}, f32[1,5]{1,0:T(1,128)}) custom-call(f32[88,128]{1,0:T(8,128)} %adjoint.1.packed_ref), custom_call_target="tpu_custom_call" | custom-call | tf_op jit(solution)/shard_map/spread/pallas_call | solution.py:574
